TPU v7x, 32 devices: a whole 2x2x4 slice. The times are simulated.
32 devices in a mesh: section: 8 (over z, x), dp: 4 (over y, core).
Axes of the slice: x: 2, y: 2, z: 4, core: 2. Of those that a mesh axis runs over, the one named last changes fastest.
Arguments:
- queries: bfloat16 [8, 1536, 1024], P('section', 'dp'), may hold values from -600 to 600
- images: bfloat16 [4, 128, 8192], P('dp', 'section'), may hold values from -6 to 6
- w_key: bfloat16 [8, 8192, 128], P('section', 'dp'), may hold values from -0.0625 to 0.0625
- w_value: bfloat16 [8, 8192, 128], P('section', 'dp'), may hold values from -0.0625 to 0.0625
- key_gain: float32 [2, 128], replicated, may hold values from 0.1 to 1.9
- d_out: bfloat16 [8, 1536, 1024], P('section', 'dp'), may hold values from -6 to 6
- img_len: int32 [4], P('dp'), may hold values from 32 to 128, as said below
- text_start: int32 [4], P('dp'), may hold values from 0 to 191
Outputs:
- attended: bfloat16 [8, 1536, 1024], P('section', 'dp')
- d_images: float32 [4, 128, 8192], P('dp', 'section')
Inputs may be any that keep to these rules, and one draw needn't show every extreme that they name: `img_len`: each sample uses a whole number of tiles of 32 tokens, 1 to 4 tiles; some sample uses all 4.
All inputs are finite; a program needn't handle non-finite values.
Results may differ from a plain program's by a relative error of at most 0.025.
Values may be sent and summed in bfloat16 or wider, within the bound.
A program may use at most 64 MiB of HBM per device.

v0:
```python
import math

import jax
import jax.numpy as jnp
from jax import lax
from jax.sharding import PartitionSpec as P

KVH = 4


def attend(key_raw, value_raw, key_gain, queries, length, start):
    inverse = lax.rsqrt(jnp.mean(key_raw * key_raw, axis=-1, keepdims=True) + 1e-05)
    keys = (key_raw * inverse * key_gain).astype(jnp.bfloat16)
    values = value_raw.astype(jnp.bfloat16)
    head_size = key_gain.shape[-1]
    heads = queries.reshape(queries.shape[0], -1, head_size).astype(jnp.float32)
    scores = jnp.einsum("thd,jd->htj", heads, keys.astype(jnp.float32)) / math.sqrt(head_size)
    usable = jnp.arange(keys.shape[0]) < length
    scores = jnp.where(usable, scores, -1e30)
    scores = scores - jnp.max(scores, axis=-1, keepdims=True)
    expo = jnp.exp(scores)
    probs = (expo / jnp.sum(expo, axis=-1, keepdims=True)).astype(jnp.bfloat16)
    mixed = jnp.einsum("htj,jd->thd", probs.astype(jnp.float32), values.astype(jnp.float32))
    mixed = mixed.reshape(queries.shape[0], -1)
    shown = jnp.arange(queries.shape[0]) >= start
    return jnp.where(shown[:, None], mixed, 0.0)


def local(queries, images, w_key, w_value, key_gain, d_out, img_len, text_start):
    image_full = lax.all_gather(images[0], "section", axis=0, tiled=True)
    key_part = w_key[0]
    value_part = w_value[0]
    layer = lax.axis_index("section") // KVH
    gain = lax.dynamic_index_in_dim(key_gain, layer, 0, keepdims=False)
    key_weight, value_weight = (
        lax.all_gather(key_part, "dp", axis=0, tiled=True),
        lax.all_gather(value_part, "dp", axis=0, tiled=True),
    )
    key_raw = jnp.dot(image_full, key_weight, preferred_element_type=jnp.float32)
    value_raw = jnp.dot(image_full, value_weight, preferred_element_type=jnp.float32)
    query_rows = queries[0]
    length = img_len[0]
    start_row = text_start[0]
    mixed, pull_back = jax.vjp(
        lambda kr, vr: attend(kr, vr, gain, query_rows, length, start_row), key_raw, value_raw
    )
    d_key, d_value = pull_back(d_out[0].astype(jnp.float32))
    d_key_half = d_key.astype(jnp.bfloat16)
    d_value_half = d_value.astype(jnp.bfloat16)
    term = jnp.dot(d_key_half, key_weight.T, preferred_element_type=jnp.float32)
    own_grads = lax.psum_scatter(
        (term + jnp.dot(d_value_half, value_weight.T, preferred_element_type=jnp.float32)).astype(
            jnp.bfloat16
        ),
        "section",
        scatter_dimension=0,
        tiled=True,
    ).astype(jnp.float32)
    return (mixed.astype(jnp.bfloat16)[None], own_grads[None])


def solution(mesh):
    return jax.shard_map(
        local,
        mesh=mesh,
        in_specs=(
            P("section", "dp", None),
            P("dp", "section", None),
            P("section", "dp", None),
            P("section", "dp", None),
            P(),
            P("section", "dp", None),
            P("dp"),
            P("dp"),
        ),
        out_specs=(P("section", "dp", None), P("dp", "section", None)),
        check_vma=False,
    )
```

profile of v0, /device:TPU:0, one launch (start us, length us, event | category | flops | bytes accessed | tf_op | source)
XLA Modules:
  0.0 199.8 jit_solution(8980685976757160952)
XLA Ops:
  7.2 0.0 copy-start
  7.2 0.0 copy-start.2
  7.2 0.0 all-gather.11.cloned.1.call-start
  7.2 0.7 all-gather.11.cloned.1.call-update
  7.9 0.0 all-gather.7.cloned.1.call-start
  8.0 0.7 all-gather.7.cloned.1.call-update
  8.7 0.0 all-gather.9.cloned.1.call-start
  8.7 0.7 all-gather.9.cloned.1.call-update
  9.4 0.0 reduce-scatter.2.cloned.1.call-start
  9.5 0.4 copy.23
  11.2 0.0 copy-done.3
  11.2 0.4 copy.22
  11.6 0.0 copy-done
  11.6 23.3 %all-gather.11.cloned.1.call-done = bf16[1,8192,128]{2,1,0:T(8,128)(2,1)} async-done(((bf16[1,2048,128]{2,1,0:T(8,128)(2,1)}), bf16[1,8192,128]{2,1,0:T(8,128)(2,1)}) %all-gather.11.cloned.1.call-update) | async-done | bytes 2097168 | tf_op jit(solution)/shard_map/all_gather | solution.py:36
  34.9 51.4 %all-gather.7.cloned.1.call-done = bf16[1,128,8192]{2,1,0:T(8,128)(2,1)} async-done(((bf16[1,16,8192]{2,1,0:T(8,128)(2,1)}), bf16[1,128,8192]{2,1,0:T(8,128)(2,1)}) %all-gather.7.cloned.1.call-update) | async-done | bytes 2097168 | tf_op jit(solution)/shard_map/all_gather | solution.py:30
  86.4 3.2 %multiply_reduce_fusion.1 = (f32[128]{0:T(128)S(1)}, f32[128,128]{0,1:T(8,128)S(1)}) fusion(bf16[1,8192,128]{2,1,0:T(8,128)(2,1)} %all-gather.11.cloned.1.call-done, bf16[1,128,8192]{2,1,0:T(8,128)(2,1)} %all-gather.7.cloned.1.call-done), kind=kOutput, calls=%fused_computation.67 | convolution fusion | flops 268468096 | bytes 4260352 | tf_op jit(solution)/shard_map/dot_general | solution.py:39
  89.5 0.5 bitcast_reduce_fusion
  90.0 0.2 fusion.64
  90.3 18.8 %all-gather.9.cloned.1.call-done = bf16[1,8192,128]{2,1,0:T(8,128)(2,1)} async-done(((bf16[1,2048,128]{2,1,0:T(8,128)(2,1)}), bf16[1,8192,128]{2,1,0:T(8,128)(2,1)}) %all-gather.9.cloned.1.call-update) | async-done | bytes 2097168 | tf_op jit(solution)/shard_map/all_gather | solution.py:37
  109.0 2.9 %fusion.57 = bf16[128,128,1]{1,0,2:T(8,128)(2,1)S(1)} fusion(bf16[1,8192,128]{2,1,0:T(8,128)(2,1)} %all-gather.9.cloned.1.call-done, bf16[1,128,8192]{2,1,0:T(8,128)(2,1)} %all-gather.7.cloned.1.call-done), kind=kOutput, calls=%fused_computation.49 | convolution fusion | flops 268451840 | bytes 4227072 | tf_op jit(solution)/shard_map/dot_general | solution.py:40
  112.0 0.5 fusion.17
  112.5 0.6 fusion.25
  113.2 0.9 multiply_reduce_fusion
  114.1 0.6 copy-done.1
  114.8 2.7 %fusion.1 = f32[128,8192]{1,0:T(8,128)} fusion(bf16[1,8192,128]{2,1,0:T(8,128)(2,1)S(1)} %copy-done.1, f32[128,128]{0,1:T(8,128)S(1)} %get-tuple-element.7, f32[128,128]{0,1:T(8,128)S(1)} %get-tuple-element.13, f32[128]{0:T(128)S(1)} %multiply_multiply_fusion, f32[128]{0:T(128)S(1)} %fusion.86), kind=kOutput, calls=%fused_computation.5 | convolution fusion | flops 268517376 | bytes 6423552 | tf_op jit(solution)/shard_map/dot_general | solution.py:50
  117.4 5.6 %fusion = bf16[128,8192]{1,0:T(8,128)(2,1)} fusion(f32[128,8192]{1,0:T(8,128)} %fusion.1, bf16[1,8192,128]{2,1,0:T(8,128)(2,1)} %all-gather.9.cloned.1.call-done, bf16[384,8,128]{0,2,1:T(8,128)(2,1)S(1)} %bitcast.133, pred[384]{0:T(512)(128)(4,1)S(1)} %iota_compare_fusion, f32[128,384,8]{1,0,2:T(8,128)S(1)} %get-tuple-element.9, f32[8,384]{1,0:T(8,128)S(1)} %fusion.64, ...), kind=kOutput, calls=%fused_computation.1 | convolution fusion | flops 372768768 | bytes 10772864 | tf_op jit(solution)/shard_map/dot_general | solution.py:52
  123.0 0.0 reduce-scatter.2.cloned.1.call-update
  123.0 0.4 fusion.92
  123.5 0.3 copy.14
  123.8 1.1 select_convert_fusion
  124.9 66.6 %reduce-scatter.2.cloned.1.call-done = bf16[16,8192]{1,0:T(8,128)(2,1)} async-done(((bf16[128,8192]{1,0:T(8,128)(2,1)}), bf16[16,8192]{1,0:T(8,128)(2,1)}) %reduce-scatter.2.cloned.1.call-update) | async-done | bytes 262160 | tf_op jit(solution)/shard_map/reduce_scatter | solution.py:51
  191.5 1.8 bitcast_convert_fusion
  (11 shorter events, 0.1 us)
Async XLA Ops:
  7.2 4.4 %copy-start = (f32[2,128]{1,0:T(2,128)S(1)}, f32[2,128]{1,0:T(2,128)}, u32[]{:S(2)}) copy-start(f32[2,128]{1,0:T(2,128)} %param.12) | copy-start | bytes 3076
  7.2 2.3 %copy-start.2 = (bf16[1,384,1024]{2,1,0:T(8,128)(2,1)S(1)}, bf16[1,384,1024]{2,1,0:T(8,128)(2,1)}, u32[]{:S(2)}) copy-start(bf16[1,384,1024]{2,1,0:T(8,128)(2,1)} %param.8) | copy-start | bytes 2359300
  7.2 4.0 %copy-start.3 = (bf16[1,384,1024]{2,1,0:T(8,128)(2,1)S(1)}, bf16[1,384,1024]{2,1,0:T(8,128)(2,1)}, u32[]{:S(2)}) copy-start(bf16[1,384,1024]{2,1,0:T(8,128)(2,1)} %param.13) | copy-start | bytes 2359300
  7.2 27.7 %all-gather.11.cloned.1.call-start = ((), (), s32[]{:S(2)}) async-start(), calls=%async_computation.4 | async-start | bytes 2621440 | tf_op jit(solution)/shard_map/all_gather | solution.py:36
  7.9 78.4 %all-gather.7.cloned.1.call-start = ((), (), s32[]{:S(2)}) async-start(), calls=%async_computation.2 | async-start | bytes 2359296 | tf_op jit(solution)/shard_map/all_gather | solution.py:30
  8.7 100.4 %all-gather.9.cloned.1.call-start = ((), (), s32[]{:S(2)}) async-start(), calls=%async_computation.3 | async-start | bytes 2621440 | tf_op jit(solution)/shard_map/all_gather | solution.py:37
  9.4 182.1 %reduce-scatter.2.cloned.1.call-start = ((), (), s32[]{:S(2)}) async-start(), calls=%async_computation.1 | async-start | bytes 2359296 | tf_op jit(solution)/shard_map/reduce_scatter | solution.py:51
  113.2 1.6 copy-start.1
Sparse Core Ops, SparseCore 0:
  9.6 25.2 all-gather.10
  37.0 49.2 all-gather.6
  87.9 21.0 all-gather.8
  123.1 68.2 reduce-scatter.1
where the time goes:
time: 200 us
  waiting for transfers between devices  162 us (81%)
  matrix products  16.7 us (8%)
  between operations  15.2 us (8%)
  other arithmetic  3.77 us (2%)
    reduce_scatter x1, waiting for transfers between devices, local(): lax.psum_scatter((term + jnp.dot(d_value_half, value_weight.T, preferred_...  66.6 us
    all_gather x1, waiting for transfers between devices, local(): image_full = lax.all_gather(images[0], 'section', axis=0, tiled=True)  51.4 us
    all_gather x1, waiting for transfers between devices, local(): lax.all_gather(key_part, 'dp', axis=0, tiled=True)  23.3 us
    all_gather x1, waiting for transfers between devices, local(): lax.all_gather(value_part, 'dp', axis=0, tiled=True)  18.8 us
    dot_general x1, matrix products, local(): jnp.dot(d_value_half, value_weight.T, preferred_element_type=jnp.float32)  5.58 us
  transfers between devices with their start and end apart: 4, of which 4 were waited for; matrix products, arithmetic and copies ran while one was open for 3% of the time, Pallas kernels for 0%

commit v1 on v0

v1 whole, which is shorter than its diff:
```python
import functools
import math

import jax
import jax.numpy as jnp
from jax import lax
from jax.experimental import pallas as pl
from jax.experimental.pallas import tpu as pltpu
from jax.sharding import PartitionSpec as P

MESH = pl.DeviceIdType.MESH
PARTS = 2
BF = jnp.bfloat16
F32 = jnp.float32


def attend(key_raw, value_raw, key_gain, queries, length, start):
    inverse = lax.rsqrt(jnp.mean(key_raw * key_raw, axis=-1, keepdims=True) + 1e-05)
    keys = (key_raw * inverse * key_gain).astype(jnp.bfloat16)
    values = value_raw.astype(jnp.bfloat16)
    head_size = key_gain.shape[-1]
    heads = queries.reshape(queries.shape[0], -1, head_size).astype(jnp.float32)
    scores = jnp.einsum("thd,jd->htj", heads, keys.astype(jnp.float32)) / math.sqrt(head_size)
    usable = jnp.arange(keys.shape[0]) < length
    scores = jnp.where(usable, scores, -1e30)
    scores = scores - jnp.max(scores, axis=-1, keepdims=True)
    expo = jnp.exp(scores)
    probs = (expo / jnp.sum(expo, axis=-1, keepdims=True)).astype(jnp.bfloat16)
    mixed = jnp.einsum("htj,jd->thd", probs.astype(jnp.float32), values.astype(jnp.float32))
    mixed = mixed.reshape(queries.shape[0], -1)
    shown = jnp.arange(queries.shape[0]) >= start
    return jnp.where(shown[:, None], mixed, 0.0)


def plain(layer_heads, queries, images, w_key, w_value, key_gain, d_out, img_len, text_start):
    image_full = lax.all_gather(images[0], "section", axis=0, tiled=True)
    layer = lax.axis_index("section") // layer_heads
    gain = lax.dynamic_index_in_dim(key_gain, layer, 0, keepdims=False)
    key_weight = lax.all_gather(w_key[0], "dp", axis=0, tiled=True)
    value_weight = lax.all_gather(w_value[0], "dp", axis=0, tiled=True)
    key_raw = jnp.dot(image_full, key_weight, preferred_element_type=jnp.float32)
    value_raw = jnp.dot(image_full, value_weight, preferred_element_type=jnp.float32)
    mixed, pull_back = jax.vjp(
        lambda kr, vr: attend(kr, vr, gain, queries[0], img_len[0], text_start[0]), key_raw, value_raw
    )
    d_key, d_value = pull_back(d_out[0].astype(jnp.float32))
    term = jnp.dot(d_key.astype(BF), key_weight.T, preferred_element_type=jnp.float32)
    term = term + jnp.dot(d_value.astype(BF), value_weight.T, preferred_element_type=jnp.float32)
    own = lax.psum_scatter(term.astype(BF), "section", scatter_dimension=0, tiled=True)
    return mixed.astype(BF)[None], own.astype(jnp.float32)[None]


def nt(a, b):
    return lax.dot_general(a, b, (((1,), (1,)), ((), ())), preferred_element_type=F32)


def kernel(
    n, m, layer_heads,
    len_ref, start_ref, gain_ref, q_hbm, img_hbm, wk_hbm, wv_hbm, do_hbm,
    att_ref, grad_ref,
    img, wk, wv, q, do, probs, term, stage, recv, kraw, vraw, dk, dv,
    local_sem, ag_send, ag_recv, w_send, w_recv, rs_send, rs_recv,
):
    half = n // 2
    s = lax.axis_index("section")
    g = lax.axis_index("dp")
    x = lax.rem(s, 2)
    pos = (1 - x) * lax.div(s, 2) + x * (n - 1 - lax.div(s, 2))

    def sec(offset):
        at = lax.rem(pos + offset + n, n)
        hi = lax.div(at, half)
        return (1 - hi) * 2 * at + hi * (2 * (n - 1 - at) + 1)

    def dp_flip(bit):
        return g + bit - 2 * bit * lax.rem(lax.div(g, bit), 2)

    def dp_xor(mask):
        at = g
        for k in range(m.bit_length() - 1):
            if mask & (1 << k):
                at = at + (1 << k) - 2 * (1 << k) * lax.rem(lax.div(g, 1 << k), 2)
        return at

    bits = [1 << k for k in reversed(range(m.bit_length() - 1))]
    right, left = sec(1), sec(-1)
    barrier = pltpu.get_barrier_semaphore()
    for neighbour in (left, right):
        pl.semaphore_signal(barrier, inc=1, device_id={"section": neighbour}, device_id_type=MESH)
    for bit in bits:
        pl.semaphore_signal(barrier, inc=1, device_id={"dp": dp_flip(bit)}, device_id_type=MESH)

    locals_ = [
        pltpu.make_async_copy(img_hbm.at[0], img.at[s], local_sem.at[0]),
        pltpu.make_async_copy(wk_hbm.at[0], wk.at[g], local_sem.at[1]),
        pltpu.make_async_copy(wv_hbm.at[0], wv.at[g], local_sem.at[2]),
        pltpu.make_async_copy(q_hbm.at[0], q, local_sem.at[3]),
        pltpu.make_async_copy(do_hbm.at[0], do, local_sem.at[4]),
    ]
    for copy in locals_:
        copy.start()
    pl.semaphore_wait(barrier, 2 + len(bits))

    cols = img.shape[2]
    part = cols // PARTS
    to = (right, left)

    def ag_copy(way, step, c):
        block = sec(-step if way == 0 else step)
        here = pl.ds(c * part, part)
        source = img_hbm.at[0, :, here] if step == 0 else img.at[block, :, here]
        return pltpu.make_async_remote_copy(
            src_ref=source,
            dst_ref=img.at[block, :, here],
            send_sem=ag_send.at[way, step, c],
            recv_sem=ag_recv.at[way, step, c],
            device_id={"section": to[way]},
            device_id_type=MESH,
        )

    def ag_arrival(way, step, c):
        block = sec(-step - 1 if way == 0 else step + 1)
        here = pl.ds(c * part, part)
        return pltpu.make_async_remote_copy(
            src_ref=img.at[block, :, here],
            dst_ref=img.at[block, :, here],
            send_sem=ag_send.at[way, step, c],
            recv_sem=ag_recv.at[way, step, c],
            device_id={"section": to[way]},
            device_id_type=MESH,
        )

    def ag_parts(way, step):
        if step < half - 1:
            return range(PARTS)
        cut = PARTS // 2
        return range(cut) if way == 0 else range(cut, PARTS)

    w_list = []
    held = [0]
    for stage_at, bit in enumerate(bits):
        for mask in list(held):
            for which in range(2):
                w_list.append((stage_at, bit, mask, which))
            held.append(mask | bit)
    w_index = {(bit, mask, which): k for k, (_, bit, mask, which) in enumerate(w_list)}

    def w_copy(bit, mask, which):
        k = w_index[(bit, mask, which)]
        block = dp_xor(mask)
        full, mine = ((wk, wk_hbm), (wv, wv_hbm))[which]
        return pltpu.make_async_remote_copy(
            src_ref=mine.at[0] if mask == 0 else full.at[block],
            dst_ref=full.at[block],
            send_sem=w_send.at[k],
            recv_sem=w_recv.at[k],
            device_id={"dp": dp_flip(bit)},
            device_id_type=MESH,
        )

    def w_arrival(bit, mask, which):
        k = w_index[(bit, mask, which)]
        block = dp_xor(mask | bit)
        full = (wk, wv)[which]
        return pltpu.make_async_remote_copy(
            src_ref=full.at[block],
            dst_ref=full.at[block],
            send_sem=w_send.at[k],
            recv_sem=w_recv.at[k],
            device_id={"dp": dp_flip(bit)},
            device_id_type=MESH,
        )

    for bit in bits:
        if bit == bits[0]:
            for which in range(2):
                w_copy(bit, 0, which).start()
    for c in range(PARTS):
        for way in range(2):
            if c in ag_parts(way, 0):
                ag_copy(way, 0, c).start()
    for bit in bits[1:]:
        for which in range(2):
            w_copy(bit, 0, which).start()
    for step in range(1, half):
        for c in range(PARTS):
            for way in range(2):
                if c in ag_parts(way, step - 1):
                    ag_arrival(way, step - 1, c).wait_recv()
                    if c in ag_parts(way, step):
                        ag_copy(way, step, c).start()
    for way in range(2):
        for c in ag_parts(way, half - 1):
            ag_arrival(way, half - 1, c).wait_recv()
    for copy in locals_:
        copy.wait()

    depth = wk.shape[1]
    tokens = n * img.shape[1]

    def project(mask, which):
        block = dp_xor(mask)
        columns = pl.ds(pl.multiple_of(block * depth, depth), depth)
        rows = img[:, :, columns].reshape(tokens, depth)
        full, raw = ((wk, kraw), (wv, vraw))[which]
        value = jnp.dot(rows, full[block], preferred_element_type=F32)
        if mask == 0:
            raw[...] = value
        else:
            raw[...] += value

    for which in range(2):
        project(0, which)
    pending = []
    for bit in reversed(bits):
        lower = [b for b in bits if b < bit]
        for which in range(2):
            w_arrival(bit, 0, which).wait_recv()
            for low in lower:
                w_copy(low, bit, which).start()
            project(bit, which)
    for stage_at, bit, mask, which in w_list:
        if mask:
            pending.append((bit, mask, which))
    for bit, mask, which in pending:
        w_arrival(bit, mask, which).wait_recv()
        for low in [b for b in bits if b < bit]:
            w_copy(low, mask | bit, which).start()
        project(mask | bit, which)

    size = kraw.shape[1]
    text = q.shape[0]
    heads = q.shape[1] // size
    layer = lax.div(s, layer_heads)
    gain = gain_ref[pl.ds(layer, 1), :]
    key_raw = kraw[...]
    inverse = lax.rsqrt(jnp.mean(key_raw * key_raw, axis=-1, keepdims=True) + 1e-05)
    keys = (key_raw * inverse * gain).astype(BF)
    values = vraw[...].astype(BF)
    usable = lax.broadcasted_iota(jnp.int32, (tokens, text), 0) < len_ref[0]
    shown = lax.broadcasted_iota(jnp.int32, (1, text), 1) >= start_ref[0]
    scale = 1.0 / math.sqrt(size)
    scale2 = scale * math.log2(math.e)
    dk[...] = jnp.zeros_like(dk)
    dv[...] = jnp.zeros_like(dv)

    def one_head(h):
        at = pl.ds(pl.multiple_of(h * size, size), size)
        qh = q[:, at]
        doh = do[:, at]
        scores = jnp.where(usable, nt(keys, qh) * scale2, -1e30)
        expo = jnp.exp2(scores - jnp.max(scores, axis=0, keepdims=True))
        factor = jnp.where(shown, 1.0 / jnp.sum(expo, axis=0, keepdims=True), 0.0)
        p = expo * factor
        half_p = p.astype(BF)
        probs[h] = half_p
        d_p = nt(values, doh).astype(BF).astype(F32)
        d_s = (p * (d_p - jnp.sum(p * d_p, axis=0, keepdims=True))).astype(BF)
        return (
            jnp.dot(d_s, qh, preferred_element_type=F32),
            jnp.dot(half_p, doh, preferred_element_type=F32),
        )

    def pair(i, carry):
        k0, v0 = one_head(2 * i)
        k1, v1 = one_head(2 * i + 1)
        dk[...] += k0 + k1
        dv[...] += v0 + v1
        return carry

    lax.fori_loop(0, heads // 2, pair, 0)
    d_keys = (dk[...] * scale).astype(BF).astype(F32) * gain
    d_key = inverse * (d_keys - key_raw * (inverse * inverse) * jnp.mean(d_keys * key_raw, axis=-1, keepdims=True))
    d_key = d_key.astype(BF)
    d_value = dv[...].astype(BF)

    rows = img.shape[1]
    first = (list(range(m // 2)), list(range(m // 2, m)))
    later = (first[1] + first[0], first[0] + first[1])

    def rs_copy(way, step, c, source):
        here = pl.ds(c * depth, depth)
        return pltpu.make_async_remote_copy(
            src_ref=source.at[:, here],
            dst_ref=recv.at[way, step, :, here],
            send_sem=rs_send.at[way, step, c],
            recv_sem=rs_recv.at[way, step, c],
            device_id={"section": to[way]},
            device_id_type=MESH,
        )

    def target(way, step):
        return sec(half - step if way == 0 else step - half)

    order = [c for both in zip(*first) for c in both]
    for c in order:
        here = pl.ds(c * depth, depth)
        value = nt(d_key, wk[c]) + nt(d_value, wv[c])
        term[:, :, here] = value.astype(BF).reshape(n, rows, depth)
        for way in range(2):
            step = 0 if c in first[way] else 1
            if step < half:
                rs_copy(way, step, c, term.at[target(way, step)]).start()

    def mix(h):
        at = pl.ds(h * size, size)
        att_ref[0, :, at] = lax.dot_general(
            probs[h], values, (((0,), (0,)), ((), ())), preferred_element_type=F32
        ).astype(BF)

    to_mix = list(range(heads))
    for step in range(1, half):
        for k in range(m):
            if to_mix:
                mix(to_mix.pop(0))
            for way in range(2):
                c = later[way][k]
                if step == 1 and c not in first[way]:
                    continue
                here = pl.ds(c * depth, depth)
                rs_copy(way, step - 1, c, stage.at[way, step]).wait_recv()
                total = term[target(way, step), :, here].astype(F32) + recv[way, step - 1, :, here].astype(F32)
                stage[way, step, :, here] = total.astype(BF)
                rs_copy(way, step, c, stage.at[way, step]).start()
    while to_mix:
        mix(to_mix.pop(0))
    last = half - 1
    for k in range(m):
        for c in (later[0][k],):
            here = pl.ds(c * depth, depth)
            grad_ref[0, :, here] = term[s, :, here].astype(F32)
    for k in range(m):
        for way in range(2):
            c = later[way][k]
            here = pl.ds(c * depth, depth)
            rs_copy(way, last, c, stage.at[way, last]).wait_recv()
            grad_ref[0, :, here] += recv[way, last, :, here].astype(F32)

    for step in range(half):
        for way in range(2):
            for c in ag_parts(way, step):
                ag_copy(way, step, c).wait_send()
    for stage_at, bit, mask, which in w_list:
        w_copy(bit, mask, which).wait_send()
    for step in range(half):
        for way in range(2):
            for c in first[way] if step == 0 else range(m):
                own = step == 0 or (step == 1 and c not in first[way])
                source = term.at[target(way, step)] if own else stage.at[way, step]
                rs_copy(way, step, c, source).wait_send()


def fused(n, m, layer_heads, queries, images, w_key, w_value, key_gain, d_out, img_len, text_start):
    _, text, width = queries.shape
    _, rows, d = images.shape
    _, depth, size = w_key.shape
    half = n // 2
    tokens = n * rows
    copies = 2 * (m - 1)
    anywhere = pl.BlockSpec(memory_space=pl.ANY)
    scalar = pl.BlockSpec(memory_space=pltpu.SMEM)
    vmem = pl.BlockSpec(memory_space=pltpu.VMEM)
    dma = pltpu.SemaphoreType.DMA
    return pl.pallas_call(
        functools.partial(kernel, n, m, layer_heads),
        out_shape=(
            jax.ShapeDtypeStruct((1, text, width), BF),
            jax.ShapeDtypeStruct((1, rows, d), F32),
        ),
        in_specs=[scalar, scalar, vmem] + [anywhere] * 5,
        out_specs=(vmem, vmem),
        scratch_shapes=[
            pltpu.VMEM((n, rows, d), BF),
            pltpu.VMEM((m, depth, size), BF),
            pltpu.VMEM((m, depth, size), BF),
            pltpu.VMEM((text, width), BF),
            pltpu.VMEM((text, width), BF),
            pltpu.VMEM((width // size, tokens, text), BF),
            pltpu.VMEM((n, rows, d), BF),
            pltpu.VMEM((2, half, rows, d), BF),
            pltpu.VMEM((2, half, rows, d), BF),
            pltpu.VMEM((tokens, size), F32),
            pltpu.VMEM((tokens, size), F32),
            pltpu.VMEM((tokens, size), F32),
            pltpu.VMEM((tokens, size), F32),
            dma((5,)),
            dma((2, half, PARTS)),
            dma((2, half, PARTS)),
            dma((copies,)),
            dma((copies,)),
            dma((2, half, m)),
            dma((2, half, m)),
        ],
        compiler_params=pltpu.CompilerParams(
            collective_id=0, has_side_effects=True, vmem_limit_bytes=40 * 1024 * 1024
        ),
    )(img_len, text_start, key_gain, queries, images, w_key, w_value, d_out)


def solution(mesh):
    n, m = mesh.shape["section"], mesh.shape["dp"]

    def local(queries, images, w_key, w_value, key_gain, d_out, img_len, text_start):
        layer_heads = n * w_key.shape[0] // key_gain.shape[0]
        rows = images.shape[1]
        depth, size = w_key.shape[1:]
        heads = queries.shape[2] // size
        fits = (
            rows % 16 == 0 and depth % 128 == 0 and n >= 4 and n % 2 == 0
            and m == 4 and heads % 2 == 0
        )
        form = functools.partial(fused, n, m) if fits else plain
        return form(layer_heads, queries, images, w_key, w_value, key_gain, d_out, img_len, text_start)

    return jax.shard_map(
        local,
        mesh=mesh,
        in_specs=(
            P("section", "dp", None),
            P("dp", "section", None),
            P("section", "dp", None),
            P("section", "dp", None),
            P(),
            P("section", "dp", None),
            P("dp"),
            P("dp"),
        ),
        out_specs=(P("section", "dp", None), P("dp", "section", None)),
        check_vma=False,
    )
```

time: 200 us -> 64.7 us (0.32)
  waiting for transfers between devices: 162 us -> 0 us
  Pallas kernels: 0 us -> 54.7 us
  matrix products: 16.7 us -> 0 us
  between operations: 15.2 us -> 1.97 us
  local copies, waits for them, and re-layouts: 1.67 us -> 6.98 us
  other arithmetic: 3.77 us -> 0 us
    all_gather x3 -> x0, waiting for transfers between devices: 93.5 us -> none  [the longest x1 51.4 us: local(): image_full = lax.all_gather(images[0], 'section', axis=0, tiled=True)]
    reduce_scatter x1 -> x0, waiting for transfers between devices: 66.6 us -> none  [local(): lax.psum_scatter((term + jnp.dot(d_value_half, value_weight.T, preferred_...]
    pallas_call x0 -> x1, Pallas kernels: none -> 54.7 us  [fused(): pl.pallas_call(functools.partial(kernel, n, m, layer_heads), out_shape=(j...]
    dot_general x8 -> x0, matrix products: 16.7 us -> none  [the longest x1 5.58 us: local(): jnp.dot(d_value_half, value_weight.T, preferred_element_type=jnp.float32)]
    unnamed x8 -> x14, local copies, waits for them, and re-layouts: 0.65 us -> 6.98 us
    unnamed x4 -> x0, waiting for transfers between devices: 2.07 us -> none
  transfers between devices with their start and end apart: 4 -> 0, of which waited for: 4 -> 0; matrix products, arithmetic and copies ran while one was open for 3% -> 0% of each run, Pallas kernels for 0% -> 0%
where the time goes in v1:
time: 64.7 us; the launch traced here: 63.7 us
  Pallas kernels  54.7 us (85%)
  local copies, waits for them, and re-layouts  6.98 us (11%)
  between operations  1.97 us (3%)
    pallas_call x1, Pallas kernels, fused(): pl.pallas_call(functools.partial(kernel, n, m, layer_heads), out_shape=(j...  54.7 us
    unnamed x14, local copies, waits for them, and re-layouts  6.98 us

profile of v1, /device:TPU:0, one launch (start us, length us, event | category | flops | bytes accessed | tf_op | source)
XLA Modules:
  0.0 63.7 jit_solution(14215426958780335365)
XLA Ops:
  1.3 0.0 copy-start.5
  1.9 0.0 copy-done.5
  2.0 0.0 copy-start
  2.0 1.1 %copy-done = bf16[1,384,1024]{2,1,0:T(8,128)(2,1)S(1)} copy-done((bf16[1,384,1024]{2,1,0:T(8,128)(2,1)S(1)}, bf16[1,384,1024]{2,1,0:T(8,128)(2,1)}, u32[]{:S(2)}) %copy-start) | copy-done | bytes 786456
  3.1 0.0 copy-start.1
  3.1 1.1 %copy-done.1 = bf16[1,384,1024]{2,1,0:T(8,128)(2,1)S(1)} copy-done((bf16[1,384,1024]{2,1,0:T(8,128)(2,1)S(1)}, bf16[1,384,1024]{2,1,0:T(8,128)(2,1)}, u32[]{:S(2)}) %copy-start.1) | copy-done | bytes 786456
  4.2 0.0 copy-start.2
  4.2 1.0 %copy-done.2 = bf16[1,2048,128]{2,1,0:T(8,128)(2,1)S(1)} copy-done((bf16[1,2048,128]{2,1,0:T(8,128)(2,1)S(1)}, bf16[1,2048,128]{2,1,0:T(8,128)(2,1)}, u32[]{:S(2)}) %copy-start.2) | copy-done | bytes 524312
  5.3 0.0 copy-start.3
  5.3 1.0 %copy-done.3 = bf16[1,2048,128]{2,1,0:T(8,128)(2,1)S(1)} copy-done((bf16[1,2048,128]{2,1,0:T(8,128)(2,1)S(1)}, bf16[1,2048,128]{2,1,0:T(8,128)(2,1)}, u32[]{:S(2)}) %copy-start.3) | copy-done | bytes 524312
  6.3 0.0 copy-start.4
  6.3 0.9 %copy-done.4 = bf16[1,16,8192]{2,1,0:T(8,128)(2,1)S(1)} copy-done((bf16[1,16,8192]{2,1,0:T(8,128)(2,1)S(1)}, bf16[1,16,8192]{2,1,0:T(8,128)(2,1)}, u32[]{:S(2)}) %copy-start.4) | copy-done | bytes 262168
  7.3 54.7 %shard_map.95 = (bf16[1,384,1024]{2,1,0:T(8,128)(2,1)S(1)}, f32[1,16,8192]{2,1,0:T(8,128)S(1)}) custom-call(s32[1]{0:T(128)S(6)} %copy.12.len_ref, s32[1]{0:T(128)S(6)} %copy.13.start_ref, f32[2,128]{1,0:T(2,128)S(1)} %copy-done.5, bf16[1,384,1024]{2,1,0:T(8,128)(2,1)S(1)} %copy-done, bf16[1,16,8192]{2,1,0:T(8,128)(2,1)S(1)} %copy-done.4, ...), custom_call_target="tpu_custom_call" | custom-call | tf_op jit(solution)/shard_map/pallas_call | solution.py:364
  62.0 0.9 %copy.14 = bf16[1,384,1024]{2,1,0:T(8,128)(2,1)} copy(bf16[1,384,1024]{2,1,0:T(8,128)(2,1)S(1)} %get-tuple-element.4) | data formatting | bytes 1572864
  62.9 0.8 %copy.15 = f32[1,16,8192]{2,1,0:T(8,128)} copy(f32[1,16,8192]{2,1,0:T(8,128)S(1)} %get-tuple-element.5) | data formatting | bytes 1048576
Async XLA Ops:
  1.3 0.7 %copy-start.5 = (f32[2,128]{1,0:T(2,128)S(1)}, f32[2,128]{1,0:T(2,128)}, u32[]{:S(2)}) copy-start(f32[2,128]{1,0:T(2,128)} %gain_ref.1) | copy-start | bytes 3076
  2.0 1.1 %copy-start = (bf16[1,384,1024]{2,1,0:T(8,128)(2,1)S(1)}, bf16[1,384,1024]{2,1,0:T(8,128)(2,1)}, u32[]{:S(2)}) copy-start(bf16[1,384,1024]{2,1,0:T(8,128)(2,1)} %q_hbm.1) | copy-start | bytes 2359300
  3.1 1.1 %copy-start.1 = (bf16[1,384,1024]{2,1,0:T(8,128)(2,1)S(1)}, bf16[1,384,1024]{2,1,0:T(8,128)(2,1)}, u32[]{:S(2)}) copy-start(bf16[1,384,1024]{2,1,0:T(8,128)(2,1)} %do_hbm.1) | copy-start | bytes 2359300
  4.2 1.0 %copy-start.2 = (bf16[1,2048,128]{2,1,0:T(8,128)(2,1)S(1)}, bf16[1,2048,128]{2,1,0:T(8,128)(2,1)}, u32[]{:S(2)}) copy-start(bf16[1,2048,128]{2,1,0:T(8,128)(2,1)} %wk_hbm.1) | copy-start | bytes 1572868
  5.3 1.0 %copy-start.3 = (bf16[1,2048,128]{2,1,0:T(8,128)(2,1)S(1)}, bf16[1,2048,128]{2,1,0:T(8,128)(2,1)}, u32[]{:S(2)}) copy-start(bf16[1,2048,128]{2,1,0:T(8,128)(2,1)} %wv_hbm.1) | copy-start | bytes 1572868
  6.3 0.9 %copy-start.4 = (bf16[1,16,8192]{2,1,0:T(8,128)(2,1)S(1)}, bf16[1,16,8192]{2,1,0:T(8,128)(2,1)}, u32[]{:S(2)}) copy-start(bf16[1,16,8192]{2,1,0:T(8,128)(2,1)} %img_hbm.1) | copy-start | bytes 786436

commit v2 on v1

--- a/solution.py
+++ b/solution.py
@@ -9,6 +9,7 @@
 from jax.sharding import PartitionSpec as P
 
 MESH = pl.DeviceIdType.MESH
+W_PARTS = 2
 PARTS = 2
 BF = jnp.bfloat16
 F32 = jnp.float32
@@ -56,9 +57,10 @@
 
 def kernel(
     n, m, layer_heads,
-    len_ref, start_ref, gain_ref, q_hbm, img_hbm, wk_hbm, wv_hbm, do_hbm,
-    att_ref, grad_ref,
-    img, wk, wv, q, do, probs, term, stage, recv, kraw, vraw, dk, dv,
+    len_hbm, start_hbm, gain_hbm, q_hbm, img_hbm, wk_hbm, wv_hbm, do_hbm,
+    att_out, grad_out,
+    att_ref, grad_ref, len_ref, start_ref, gain_ref,
+    img, wk, wv, q, do, exact, probs, term, stage, recv, kraw, vraw, dk, dv,
     local_sem, ag_send, ag_recv, w_send, w_recv, rs_send, rs_recv,
 ):
     half = n // 2
@@ -96,6 +98,9 @@
         pltpu.make_async_copy(wv_hbm.at[0], wv.at[g], local_sem.at[2]),
         pltpu.make_async_copy(q_hbm.at[0], q, local_sem.at[3]),
         pltpu.make_async_copy(do_hbm.at[0], do, local_sem.at[4]),
+        pltpu.make_async_copy(gain_hbm, gain_ref, local_sem.at[5]),
+        pltpu.make_async_copy(len_hbm, len_ref, local_sem.at[6]),
+        pltpu.make_async_copy(start_hbm, start_ref, local_sem.at[7]),
     ]
     for copy in locals_:
         copy.start()
@@ -136,66 +141,49 @@
         cut = PARTS // 2
         return range(cut) if way == 0 else range(cut, PARTS)
 
+    depth = wk.shape[1]
+    cut = depth // W_PARTS
     w_list = []
     held = [0]
-    for stage_at, bit in enumerate(bits):
+    for bit in bits:
         for mask in list(held):
             for which in range(2):
-                w_list.append((stage_at, bit, mask, which))
+                for c in range(W_PARTS):
+                    w_list.append((bit, mask, which, c))
             held.append(mask | bit)
-    w_index = {(bit, mask, which): k for k, (_, bit, mask, which) in enumerate(w_list)}
-
-    def w_copy(bit, mask, which):
-        k = w_index[(bit, mask, which)]
+    w_index = {item: k for k, item in enumerate(w_list)}
+
+    def w_copy(bit, mask, which, c):
+        k = w_index[(bit, mask, which, c)]
         block = dp_xor(mask)
+        here = pl.ds(c * cut, cut)
         full, mine = ((wk, wk_hbm), (wv, wv_hbm))[which]
         return pltpu.make_async_remote_copy(
-            src_ref=mine.at[0] if mask == 0 else full.at[block],
-            dst_ref=full.at[block],
+            src_ref=mine.at[0, here] if mask == 0 else full.at[block, here],
+            dst_ref=full.at[block, here],
             send_sem=w_send.at[k],
             recv_sem=w_recv.at[k],
             device_id={"dp": dp_flip(bit)},
             device_id_type=MESH,
         )
 
-    def w_arrival(bit, mask, which):
-        k = w_index[(bit, mask, which)]
-        block = dp_xor(mask | bit)
-        full = (wk, wv)[which]
-        return pltpu.make_async_remote_copy(
-            src_ref=full.at[block],
-            dst_ref=full.at[block],
+    def w_take(bit, mask, which, c):
+        k = w_index[(bit, mask, which, c)]
+        here = pl.ds(c * cut, cut)
+        landed = (wk, wv)[which].at[dp_xor(mask | bit), here]
+        pltpu.make_async_remote_copy(
+            src_ref=landed,
+            dst_ref=landed,
             send_sem=w_send.at[k],
             recv_sem=w_recv.at[k],
             device_id={"dp": dp_flip(bit)},
             device_id_type=MESH,
-        )
-
-    for bit in bits:
-        if bit == bits[0]:
-            for which in range(2):
-                w_copy(bit, 0, which).start()
-    for c in range(PARTS):
-        for way in range(2):
-            if c in ag_parts(way, 0):
-                ag_copy(way, 0, c).start()
-    for bit in bits[1:]:
-        for which in range(2):
-            w_copy(bit, 0, which).start()
-    for step in range(1, half):
-        for c in range(PARTS):
-            for way in range(2):
-                if c in ag_parts(way, step - 1):
-                    ag_arrival(way, step - 1, c).wait_recv()
-                    if c in ag_parts(way, step):
-                        ag_copy(way, step, c).start()
-    for way in range(2):
-        for c in ag_parts(way, half - 1):
-            ag_arrival(way, half - 1, c).wait_recv()
-    for copy in locals_:
-        copy.wait()
-
-    depth = wk.shape[1]
+        ).wait_recv()
+        for low in bits:
+            if low < bit:
+                w_copy(low, mask | bit, which, c).start()
+
+    far, near = bits
     tokens = n * img.shape[1]
 
     def project(mask, which):
@@ -209,24 +197,42 @@
         else:
             raw[...] += value
 
+    for c in range(W_PARTS):
+        w_copy(far, 0, 0, c).start()
+    for c in range(PARTS):
+        for way in range(2):
+            if c in ag_parts(way, 0):
+                ag_copy(way, 0, c).start()
     for which in range(2):
-        project(0, which)
-    pending = []
-    for bit in reversed(bits):
-        lower = [b for b in bits if b < bit]
-        for which in range(2):
-            w_arrival(bit, 0, which).wait_recv()
-            for low in lower:
-                w_copy(low, bit, which).start()
-            project(bit, which)
-    for stage_at, bit, mask, which in w_list:
-        if mask:
-            pending.append((bit, mask, which))
-    for bit, mask, which in pending:
-        w_arrival(bit, mask, which).wait_recv()
-        for low in [b for b in bits if b < bit]:
-            w_copy(low, mask | bit, which).start()
-        project(mask | bit, which)
+        for c in range(W_PARTS):
+            w_copy(near, 0, which, c).start()
+    for step in range(1, half):
+        for c in range(PARTS):
+            for way in range(2):
+                if c in ag_parts(way, step - 1):
+                    ag_arrival(way, step - 1, c).wait_recv()
+                    if c in ag_parts(way, step):
+                        ag_copy(way, step, c).start()
+        if step == half // 2:
+            for c in range(W_PARTS):
+                w_copy(far, 0, 0, c).wait_send()
+                w_copy(far, 0, 1, c).start()
+    for copy in locals_:
+        copy.wait()
+    for c in range(W_PARTS):
+        w_take(far, 0, 0, c)
+    for which in range(2):
+        for c in range(W_PARTS):
+            w_take(near, 0, which, c)
+    for c in range(W_PARTS):
+        w_take(near, far, 0, c)
+    for c in range(W_PARTS - 1):
+        w_take(far, 0, 1, c)
+    for way in range(2):
+        for c in ag_parts(way, half - 1):
+            ag_arrival(way, half - 1, c).wait_recv()
+    for mask in (0, near, far, far | near):
+        project(mask, 0)
 
     size = kraw.shape[1]
     text = q.shape[0]
@@ -236,39 +242,41 @@
     key_raw = kraw[...]
     inverse = lax.rsqrt(jnp.mean(key_raw * key_raw, axis=-1, keepdims=True) + 1e-05)
     keys = (key_raw * inverse * gain).astype(BF)
-    values = vraw[...].astype(BF)
     usable = lax.broadcasted_iota(jnp.int32, (tokens, text), 0) < len_ref[0]
     shown = lax.broadcasted_iota(jnp.int32, (1, text), 1) >= start_ref[0]
     scale = 1.0 / math.sqrt(size)
     scale2 = scale * math.log2(math.e)
-    dk[...] = jnp.zeros_like(dk)
-    dv[...] = jnp.zeros_like(dv)
-
-    def one_head(h):
-        at = pl.ds(pl.multiple_of(h * size, size), size)
-        qh = q[:, at]
-        doh = do[:, at]
-        scores = jnp.where(usable, nt(keys, qh) * scale2, -1e30)
+
+    def forward(h):
+        at = pl.ds(h * size, size)
+        scores = jnp.where(usable, nt(keys, q[:, at]) * scale2, -1e30)
         expo = jnp.exp2(scores - jnp.max(scores, axis=0, keepdims=True))
         factor = jnp.where(shown, 1.0 / jnp.sum(expo, axis=0, keepdims=True), 0.0)
         p = expo * factor
         half_p = p.astype(BF)
+        exact[h] = p
         probs[h] = half_p
-        d_p = nt(values, doh).astype(BF).astype(F32)
+        return jnp.dot(half_p, do[:, at], preferred_element_type=F32)
+
+    def backward(h):
+        at = pl.ds(h * size, size)
+        p = exact[h]
+        d_p = nt(values, do[:, at]).astype(BF).astype(F32)
         d_s = (p * (d_p - jnp.sum(p * d_p, axis=0, keepdims=True))).astype(BF)
-        return (
-            jnp.dot(d_s, qh, preferred_element_type=F32),
-            jnp.dot(half_p, doh, preferred_element_type=F32),
-        )
-
-    def pair(i, carry):
-        k0, v0 = one_head(2 * i)
-        k1, v1 = one_head(2 * i + 1)
-        dk[...] += k0 + k1
-        dv[...] += v0 + v1
-        return carry
-
-    lax.fori_loop(0, heads // 2, pair, 0)
+        return jnp.dot(d_s, q[:, at], preferred_element_type=F32)
+
+    first_heads = heads // 2
+    dv[...] = sum(forward(h) for h in range(first_heads))
+    w_take(far, 0, 1, W_PARTS - 1)
+    dv[...] += sum(forward(h) for h in range(first_heads, heads))
+    for mask in (0, near, far):
+        project(mask, 1)
+    for c in range(W_PARTS):
+        w_take(near, far, 1, c)
+    project(far | near, 1)
+    values = vraw[...].astype(BF)
+    dk[...] = sum(backward(h) for h in range(first_heads))
+    dk[...] += sum(backward(h) for h in range(first_heads, heads))
     d_keys = (dk[...] * scale).astype(BF).astype(F32) * gain
     d_key = inverse * (d_keys - key_raw * (inverse * inverse) * jnp.mean(d_keys * key_raw, axis=-1, keepdims=True))
     d_key = d_key.astype(BF)
@@ -304,7 +312,7 @@
 
     def mix(h):
         at = pl.ds(h * size, size)
-        att_ref[0, :, at] = lax.dot_general(
+        att_ref[:, at] = lax.dot_general(
             probs[h], values, (((0,), (0,)), ((), ())), preferred_element_type=F32
         ).astype(BF)
 
@@ -324,24 +332,36 @@
                 rs_copy(way, step, c, stage.at[way, step]).start()
     while to_mix:
         mix(to_mix.pop(0))
+    att_copy = pltpu.make_async_copy(att_ref, att_out.at[0], local_sem.at[0])
+    att_copy.start()
     last = half - 1
-    for k in range(m):
-        for c in (later[0][k],):
-            here = pl.ds(c * depth, depth)
-            grad_ref[0, :, here] = term[s, :, here].astype(F32)
+    grad_copies = []
+    seen = []
     for k in range(m):
         for way in range(2):
             c = later[way][k]
             here = pl.ds(c * depth, depth)
             rs_copy(way, last, c, stage.at[way, last]).wait_recv()
-            grad_ref[0, :, here] += recv[way, last, :, here].astype(F32)
-
+            value = recv[way, last, :, here].astype(F32)
+            if c not in seen:
+                seen.append(c)
+                grad_ref[:, here] = term[s, :, here].astype(F32) + value
+            else:
+                grad_ref[:, here] += value
+                copy = pltpu.make_async_copy(grad_ref.at[:, here], grad_out.at[0, :, here], local_sem.at[1 + c])
+                copy.start()
+                grad_copies.append(copy)
+
+    att_copy.wait()
+    for copy in grad_copies:
+        copy.wait()
     for step in range(half):
         for way in range(2):
             for c in ag_parts(way, step):
                 ag_copy(way, step, c).wait_send()
-    for stage_at, bit, mask, which in w_list:
-        w_copy(bit, mask, which).wait_send()
+    for bit, mask, which, c in w_list:
+        if (bit, which) != (far, 0):
+            w_copy(bit, mask, which, c).wait_send()
     for step in range(half):
         for way in range(2):
             for c in first[way] if step == 0 else range(m):
@@ -356,10 +376,8 @@
     _, depth, size = w_key.shape
     half = n // 2
     tokens = n * rows
-    copies = 2 * (m - 1)
-    anywhere = pl.BlockSpec(memory_space=pl.ANY)
-    scalar = pl.BlockSpec(memory_space=pltpu.SMEM)
-    vmem = pl.BlockSpec(memory_space=pltpu.VMEM)
+    copies = 2 * (m - 1) * W_PARTS
+    hbm = pl.BlockSpec(memory_space=pl.ANY)
     dma = pltpu.SemaphoreType.DMA
     return pl.pallas_call(
         functools.partial(kernel, n, m, layer_heads),
@@ -367,14 +385,20 @@
             jax.ShapeDtypeStruct((1, text, width), BF),
             jax.ShapeDtypeStruct((1, rows, d), F32),
         ),
-        in_specs=[scalar, scalar, vmem] + [anywhere] * 5,
-        out_specs=(vmem, vmem),
+        in_specs=[hbm] * 8,
+        out_specs=(hbm, hbm),
         scratch_shapes=[
+            pltpu.VMEM((text, width), BF),
+            pltpu.VMEM((rows, d), F32),
+            pltpu.SMEM(img_len.shape, img_len.dtype),
+            pltpu.SMEM(text_start.shape, text_start.dtype),
+            pltpu.VMEM(key_gain.shape, key_gain.dtype),
             pltpu.VMEM((n, rows, d), BF),
             pltpu.VMEM((m, depth, size), BF),
             pltpu.VMEM((m, depth, size), BF),
             pltpu.VMEM((text, width), BF),
             pltpu.VMEM((text, width), BF),
+            pltpu.VMEM((width // size, tokens, text), F32),
             pltpu.VMEM((width // size, tokens, text), BF),
             pltpu.VMEM((n, rows, d), BF),
             pltpu.VMEM((2, half, rows, d), BF),
@@ -383,7 +407,7 @@
             pltpu.VMEM((tokens, size), F32),
             pltpu.VMEM((tokens, size), F32),
             pltpu.VMEM((tokens, size), F32),
-            dma((5,)),
+            dma((8,)),
             dma((2, half, PARTS)),
             dma((2, half, PARTS)),
             dma((copies,)),
@@ -392,7 +416,7 @@
             dma((2, half, m)),
         ],
         compiler_params=pltpu.CompilerParams(
-            collective_id=0, has_side_effects=True, vmem_limit_bytes=40 * 1024 * 1024
+            collective_id=0, has_side_effects=True, vmem_limit_bytes=63 * 1024 * 1024
         ),
     )(img_len, text_start, key_gain, queries, images, w_key, w_value, d_out)
 

time: 64.7 us -> 62.3 us (0.963); the launches traced: 63.7 us -> 62.2 us
  local copies, waits for them, and re-layouts: 6.98 us -> 2.92 us
  Pallas kernels: 54.7 us -> 57.3 us
    unnamed x14 -> x4, local copies, waits for them, and re-layouts: 6.98 us -> 2.92 us
    pallas_call x1, Pallas kernels: 54.7 us -> 57.3 us  [fused(): pl.pallas_call(functools.partial(kernel, n, m, layer_heads), out_shape=(j...]
where the time goes in v2:
time: 62.3 us; the launch traced here: 62.2 us
  Pallas kernels  57.3 us (92%)
  local copies, waits for them, and re-layouts  2.92 us (5%)
  between operations  1.94 us (3%)
    pallas_call x1, Pallas kernels, fused(): pl.pallas_call(functools.partial(kernel, n, m, layer_heads), out_shape=(j...  57.3 us
    unnamed x4, local copies, waits for them, and re-layouts  2.92 us

profile of v2, /device:TPU:0, one launch (start us, length us, event | category | flops | bytes accessed | tf_op | source)
XLA Modules:
  0.0 62.2 jit_solution(15600037699122837440)
XLA Ops:
  1.9 57.3 %shard_map.95 = (bf16[1,384,1024]{2,1,0:T(8,128)(2,1)}, f32[1,16,8192]{2,1,0:T(8,128)}) custom-call(s32[1]{0:T(128)S(6)} %copy.12.len_hbm, s32[1]{0:T(128)S(6)} %copy.13.start_hbm, f32[2,128]{1,0:T(2,128)} %gain_hbm.1, bf16[1,384,1024]{2,1,0:T(8,128)(2,1)} %q_hbm.1, bf16[1,16,8192]{2,1,0:T(8,128)(2,1)} %img_hbm.1, bf16[1,2048,128]{2,1,0:T(8,128)(2,1)} %wk_hbm.1, ...), custom_call_target="tpu_custom_call" | custom-call | tf_op jit(solution)/shard_map/pallas_call | solution.py:382
  59.2 0.0 copy-start
  59.2 2.1 %copy.14 = bf16[1,384,1024]{2,1,0:T(8,128)(2,1)} copy(bf16[1,384,1024]{2,1,0:T(8,128)(2,1)} %get-tuple-element.4) | data formatting | bytes 1572864
  61.4 0.0 copy-done
  61.4 0.8 %copy.15 = f32[1,16,8192]{2,1,0:T(8,128)} copy(f32[1,16,8192]{2,1,0:T(8,128)S(1)} %copy-done) | data formatting | bytes 1048576
Async XLA Ops:
  59.2 2.1 %copy-start = (f32[1,16,8192]{2,1,0:T(8,128)S(1)}, f32[1,16,8192]{2,1,0:T(8,128)}, u32[]{:S(2)}) copy-start(f32[1,16,8192]{2,1,0:T(8,128)} %get-tuple-element.5) | copy-start | bytes 1572868

commit v3 on v2

--- a/solution.py
+++ b/solution.py
@@ -58,8 +58,8 @@
 def kernel(
     n, m, layer_heads,
     len_hbm, start_hbm, gain_hbm, q_hbm, img_hbm, wk_hbm, wv_hbm, do_hbm,
-    att_out, grad_out,
-    att_ref, grad_ref, len_ref, start_ref, gain_ref,
+    att_ref, grad_ref,
+    len_ref, start_ref, gain_ref,
     img, wk, wv, q, do, exact, probs, term, stage, recv, kraw, vraw, dk, dv,
     local_sem, ag_send, ag_recv, w_send, w_recv, rs_send, rs_recv,
 ):
@@ -213,10 +213,8 @@
                     ag_arrival(way, step - 1, c).wait_recv()
                     if c in ag_parts(way, step):
                         ag_copy(way, step, c).start()
-        if step == half // 2:
-            for c in range(W_PARTS):
-                w_copy(far, 0, 0, c).wait_send()
-                w_copy(far, 0, 1, c).start()
+        if step <= W_PARTS:
+            w_copy(far, 0, 1, step - 1).start()
     for copy in locals_:
         copy.wait()
     for c in range(W_PARTS):
@@ -312,7 +310,7 @@
 
     def mix(h):
         at = pl.ds(h * size, size)
-        att_ref[:, at] = lax.dot_general(
+        att_ref[0, :, at] = lax.dot_general(
             probs[h], values, (((0,), (0,)), ((), ())), preferred_element_type=F32
         ).astype(BF)
 
@@ -332,10 +330,7 @@
                 rs_copy(way, step, c, stage.at[way, step]).start()
     while to_mix:
         mix(to_mix.pop(0))
-    att_copy = pltpu.make_async_copy(att_ref, att_out.at[0], local_sem.at[0])
-    att_copy.start()
     last = half - 1
-    grad_copies = []
     seen = []
     for k in range(m):
         for way in range(2):
@@ -345,23 +340,16 @@
             value = recv[way, last, :, here].astype(F32)
             if c not in seen:
                 seen.append(c)
-                grad_ref[:, here] = term[s, :, here].astype(F32) + value
+                grad_ref[0, :, here] = term[s, :, here].astype(F32) + value
             else:
-                grad_ref[:, here] += value
-                copy = pltpu.make_async_copy(grad_ref.at[:, here], grad_out.at[0, :, here], local_sem.at[1 + c])
-                copy.start()
-                grad_copies.append(copy)
-
-    att_copy.wait()
-    for copy in grad_copies:
-        copy.wait()
+                grad_ref[0, :, here] += value
+
     for step in range(half):
         for way in range(2):
             for c in ag_parts(way, step):
                 ag_copy(way, step, c).wait_send()
-    for bit, mask, which, c in w_list:
-        if (bit, which) != (far, 0):
-            w_copy(bit, mask, which, c).wait_send()
+    for item in w_list:
+        w_copy(*item).wait_send()
     for step in range(half):
         for way in range(2):
             for c in first[way] if step == 0 else range(m):
@@ -382,14 +370,12 @@
     return pl.pallas_call(
         functools.partial(kernel, n, m, layer_heads),
         out_shape=(
-            jax.ShapeDtypeStruct((1, text, width), BF),
-            jax.ShapeDtypeStruct((1, rows, d), F32),
+            pltpu.VMEM((1, text, width), BF),
+            pltpu.VMEM((1, rows, d), F32),
         ),
         in_specs=[hbm] * 8,
-        out_specs=(hbm, hbm),
+        out_specs=(pl.BlockSpec(memory_space=pltpu.VMEM),) * 2,
         scratch_shapes=[
-            pltpu.VMEM((text, width), BF),
-            pltpu.VMEM((rows, d), F32),
             pltpu.SMEM(img_len.shape, img_len.dtype),
             pltpu.SMEM(text_start.shape, text_start.dtype),
             pltpu.VMEM(key_gain.shape, key_gain.dtype),
@@ -416,7 +402,7 @@
             dma((2, half, m)),
         ],
         compiler_params=pltpu.CompilerParams(
-            collective_id=0, has_side_effects=True, vmem_limit_bytes=63 * 1024 * 1024
+            collective_id=0, has_side_effects=True, vmem_limit_bytes=60 * 1024 * 1024
         ),
     )(img_len, text_start, key_gain, queries, images, w_key, w_value, d_out)
 

time: 62.3 us -> 59.4 us (0.953)
  Pallas kernels: 57.3 us -> 55.6 us
  local copies, waits for them, and re-layouts: 2.92 us -> 1.67 us
    pallas_call x1, Pallas kernels: 57.3 us -> 55.6 us  [fused(): pl.pallas_call(functools.partial(kernel, n, m, layer_heads), out_shape=(p...]
    unnamed x4 -> x2, local copies, waits for them, and re-layouts: 2.92 us -> 1.67 us
where the time goes in v3:
time: 59.4 us; the launch traced here: 59.2 us
  Pallas kernels  55.6 us (94%)
  between operations  1.93 us (3%)
  local copies, waits for them, and re-layouts  1.67 us (3%)
    pallas_call x1, Pallas kernels, fused(): pl.pallas_call(functools.partial(kernel, n, m, layer_heads), out_shape=(p...  55.6 us
    unnamed x2, local copies, waits for them, and re-layouts  1.67 us

profile of v3, /device:TPU:0, one launch (start us, length us, event | category | flops | bytes accessed | tf_op | source)
XLA Modules:
  0.0 59.2 jit_solution(16196334400095306205)
XLA Ops:
  1.9 55.6 %shard_map.95 = (bf16[1,384,1024]{2,1,0:T(8,128)(2,1)S(1)}, f32[1,16,8192]{2,1,0:T(8,128)S(1)}) custom-call(s32[1]{0:T(128)S(6)} %copy.14.len_hbm, s32[1]{0:T(128)S(6)} %copy.15.start_hbm, f32[2,128]{1,0:T(2,128)} %gain_hbm.1, bf16[1,384,1024]{2,1,0:T(8,128)(2,1)} %q_hbm.1, bf16[1,16,8192]{2,1,0:T(8,128)(2,1)} %img_hbm.1, bf16[1,2048,128]{2,1,0:T(8,128)(2,1)} %wk_hbm.1, ...), custom_call_target="tpu_custom_call" | custom-call | tf_op jit(solution)/shard_map/pallas_call | solution.py:370
  57.5 0.9 %copy.12 = bf16[1,384,1024]{2,1,0:T(8,128)(2,1)} copy(bf16[1,384,1024]{2,1,0:T(8,128)(2,1)S(1)} %get-tuple-element.2) | data formatting | bytes 1572864
  58.4 0.8 %copy.13 = f32[1,16,8192]{2,1,0:T(8,128)} copy(f32[1,16,8192]{2,1,0:T(8,128)S(1)} %get-tuple-element.3) | data formatting | bytes 1048576

commit v4 on v3

--- a/solution.py
+++ b/solution.py
@@ -186,16 +186,14 @@
     far, near = bits
     tokens = n * img.shape[1]
 
-    def project(mask, which):
+    def project(mask, which=None):
         block = dp_xor(mask)
         columns = pl.ds(pl.multiple_of(block * depth, depth), depth)
         rows = img[:, :, columns].reshape(tokens, depth)
-        full, raw = ((wk, kraw), (wv, vraw))[which]
-        value = jnp.dot(rows, full[block], preferred_element_type=F32)
-        if mask == 0:
-            raw[...] = value
-        else:
-            raw[...] += value
+        if which is None:
+            weight = jnp.concatenate([wk[block], wv[block]], axis=1)
+            return jnp.dot(rows, weight, preferred_element_type=F32)
+        return jnp.dot(rows, (wk, wv)[which][block], preferred_element_type=F32)
 
     for c in range(W_PARTS):
         w_copy(far, 0, 0, c).start()
@@ -229,10 +227,13 @@
     for way in range(2):
         for c in ag_parts(way, half - 1):
             ag_arrival(way, half - 1, c).wait_recv()
-    for mask in (0, near, far, far | near):
-        project(mask, 0)
+    both = project(0) + project(near)
+    w_take(far, 0, 1, W_PARTS - 1)
+    both = both + project(far)
 
     size = kraw.shape[1]
+    kraw[...] = both[:, :size] + project(far | near, 0)
+    vraw[...] = both[:, size:]
     text = q.shape[0]
     heads = q.shape[1] // size
     layer = lax.div(s, layer_heads)
@@ -265,20 +266,15 @@
 
     first_heads = heads // 2
     dv[...] = sum(forward(h) for h in range(first_heads))
-    w_take(far, 0, 1, W_PARTS - 1)
     dv[...] += sum(forward(h) for h in range(first_heads, heads))
-    for mask in (0, near, far):
-        project(mask, 1)
     for c in range(W_PARTS):
         w_take(near, far, 1, c)
-    project(far | near, 1)
-    values = vraw[...].astype(BF)
+    values = (vraw[...] + project(far | near, 1)).astype(BF)
     dk[...] = sum(backward(h) for h in range(first_heads))
     dk[...] += sum(backward(h) for h in range(first_heads, heads))
     d_keys = (dk[...] * scale).astype(BF).astype(F32) * gain
     d_key = inverse * (d_keys - key_raw * (inverse * inverse) * jnp.mean(d_keys * key_raw, axis=-1, keepdims=True))
-    d_key = d_key.astype(BF)
-    d_value = dv[...].astype(BF)
+    d_both = jnp.concatenate([d_key.astype(BF), dv[...].astype(BF)], axis=1)
 
     rows = img.shape[1]
     first = (list(range(m // 2)), list(range(m // 2, m)))
@@ -301,7 +297,7 @@
     order = [c for both in zip(*first) for c in both]
     for c in order:
         here = pl.ds(c * depth, depth)
-        value = nt(d_key, wk[c]) + nt(d_value, wv[c])
+        value = nt(d_both, jnp.concatenate([wk[c], wv[c]], axis=1))
         term[:, :, here] = value.astype(BF).reshape(n, rows, depth)
         for way in range(2):
             step = 0 if c in first[way] else 1

time: 59.4 us -> 58.8 us (0.990)
  Pallas kernels: 55.6 us -> 55 us
    pallas_call x1, Pallas kernels: 55.6 us -> 55 us  [fused(): pl.pallas_call(functools.partial(kernel, n, m, layer_heads), out_shape=(p...]
where the time goes in v4:
time: 58.8 us; the launch traced here: 58.6 us
  Pallas kernels  55 us (94%)
  between operations  1.93 us (3%)
  local copies, waits for them, and re-layouts  1.67 us (3%)
    pallas_call x1, Pallas kernels, fused(): pl.pallas_call(functools.partial(kernel, n, m, layer_heads), out_shape=(p...  55 us
    unnamed x2, local copies, waits for them, and re-layouts  1.67 us

profile of v4, /device:TPU:0, one launch (start us, length us, event | category | flops | bytes accessed | tf_op | source)
XLA Modules:
  0.0 58.6 jit_solution(13107603619092505298)
XLA Ops:
  1.9 55.0 %shard_map.95 = (bf16[1,384,1024]{2,1,0:T(8,128)(2,1)S(1)}, f32[1,16,8192]{2,1,0:T(8,128)S(1)}) custom-call(s32[1]{0:T(128)S(6)} %copy.14.len_hbm, s32[1]{0:T(128)S(6)} %copy.15.start_hbm, f32[2,128]{1,0:T(2,128)} %gain_hbm.1, bf16[1,384,1024]{2,1,0:T(8,128)(2,1)} %q_hbm.1, bf16[1,16,8192]{2,1,0:T(8,128)(2,1)} %img_hbm.1, bf16[1,2048,128]{2,1,0:T(8,128)(2,1)} %wk_hbm.1, ...), custom_call_target="tpu_custom_call" | custom-call | tf_op jit(solution)/shard_map/pallas_call | solution.py:366
  56.9 0.9 %copy.12 = bf16[1,384,1024]{2,1,0:T(8,128)(2,1)} copy(bf16[1,384,1024]{2,1,0:T(8,128)(2,1)S(1)} %get-tuple-element.2) | data formatting | bytes 1572864
  57.8 0.8 %copy.13 = f32[1,16,8192]{2,1,0:T(8,128)} copy(f32[1,16,8192]{2,1,0:T(8,128)S(1)} %get-tuple-element.3) | data formatting | bytes 1048576

commit v5 on v4

--- a/solution.py
+++ b/solution.py
@@ -10,7 +10,7 @@
 
 MESH = pl.DeviceIdType.MESH
 W_PARTS = 2
-PARTS = 2
+PARTS = 4
 BF = jnp.bfloat16
 F32 = jnp.float32
 
@@ -102,8 +102,6 @@
         pltpu.make_async_copy(len_hbm, len_ref, local_sem.at[6]),
         pltpu.make_async_copy(start_hbm, start_ref, local_sem.at[7]),
     ]
-    for copy in locals_:
-        copy.start()
     pl.semaphore_wait(barrier, 2 + len(bits))
 
     cols = img.shape[2]
@@ -195,15 +193,17 @@
             return jnp.dot(rows, weight, preferred_element_type=F32)
         return jnp.dot(rows, (wk, wv)[which][block], preferred_element_type=F32)
 
-    for c in range(W_PARTS):
-        w_copy(far, 0, 0, c).start()
     for c in range(PARTS):
         for way in range(2):
             if c in ag_parts(way, 0):
                 ag_copy(way, 0, c).start()
+    for c in range(W_PARTS):
+        w_copy(far, 0, 0, c).start()
     for which in range(2):
         for c in range(W_PARTS):
             w_copy(near, 0, which, c).start()
+    for copy in locals_:
+        copy.start()
     for step in range(1, half):
         for c in range(PARTS):
             for way in range(2):

time: 58.8 us -> 59.1 us (level)
  no operation moved by 1% of the time
where the time goes in v5:
time: 59.1 us; the launch traced here: 58.9 us
  Pallas kernels  55.3 us (94%)
  between operations  1.93 us (3%)
  local copies, waits for them, and re-layouts  1.67 us (3%)
    pallas_call x1, Pallas kernels, fused(): pl.pallas_call(functools.partial(kernel, n, m, layer_heads), out_shape=(p...  55.3 us
    unnamed x2, local copies, waits for them, and re-layouts  1.67 us

profile of v5, /device:TPU:0, one launch (start us, length us, event | category | flops | bytes accessed | tf_op | source)
XLA Modules:
  0.0 58.9 jit_solution(10598897824939084240)
XLA Ops:
  1.9 55.3 %shard_map.95 = (bf16[1,384,1024]{2,1,0:T(8,128)(2,1)S(1)}, f32[1,16,8192]{2,1,0:T(8,128)S(1)}) custom-call(s32[1]{0:T(128)S(6)} %copy.14.len_hbm, s32[1]{0:T(128)S(6)} %copy.15.start_hbm, f32[2,128]{1,0:T(2,128)} %gain_hbm.1, bf16[1,384,1024]{2,1,0:T(8,128)(2,1)} %q_hbm.1, bf16[1,16,8192]{2,1,0:T(8,128)(2,1)} %img_hbm.1, bf16[1,2048,128]{2,1,0:T(8,128)(2,1)} %wk_hbm.1, ...), custom_call_target="tpu_custom_call" | custom-call | tf_op jit(solution)/shard_map/pallas_call | solution.py:366
  57.2 0.9 %copy.12 = bf16[1,384,1024]{2,1,0:T(8,128)(2,1)} copy(bf16[1,384,1024]{2,1,0:T(8,128)(2,1)S(1)} %get-tuple-element.2) | data formatting | bytes 1572864
  58.1 0.8 %copy.13 = f32[1,16,8192]{2,1,0:T(8,128)} copy(f32[1,16,8192]{2,1,0:T(8,128)S(1)} %get-tuple-element.3) | data formatting | bytes 1048576
